TPU v7x, 128 devices: a whole 4x4x4 slice. The times are simulated.
128 devices in a mesh: seq: 32 (over z, x, core), dp: 4 (over y).
Axes of the slice: x: 4, y: 4, z: 4, core: 2. Of those that a mesh axis runs over, the one named last changes fastest.
Arguments:
- queries: bfloat16 [65536, 2048], P(('dp', 'seq')), parts along dimension 0, may hold values from -150 to 150
- keys_values: bfloat16 [65536, 2, 2048], P(('dp', 'seq')), parts along dimension 0, may hold values from -4.5 to 4.5
- image_tiles: int32 [64], P('dp'), parts along dimension 0, may hold values from 1 to 8, 32 in all
- loader_tiles: int32 [128], P('dp'), parts along dimension 0, may hold values from 0 to 31, each once
Outputs:
- attended: bfloat16 [65536, 2048], P(('dp', 'seq')), parts along dimension 0
There are 4 independent parts, one for each index of `dp`. A program takes and returns all parts, laid end to end along the dimension named above; each array names one. Nothing has to cross between parts.
Inputs may be any that keep to these rules, and one draw needn't show every extreme that they name: `image_tiles`: image sizes in tiles sum to 32; the largest is exactly 8. `loader_tiles`: each tile number appears once.
All inputs are finite; a program needn't handle non-finite values.
Results may differ from a plain program's by a relative error of at most 0.006.
Values may be sent and summed in bfloat16 or wider, within the bound.
A program may use at most 128 MiB of HBM per device.

v0:
```python
import jax
import jax.numpy as jnp
from jax import lax
from jax.sharding import PartitionSpec as P

HD = 128


def local(queries, keys_values, image_tiles, loader_tiles):
    seq_devices = lax.axis_size("seq")
    halves = 2
    groups = seq_devices // halves
    tile_rows = queries.shape[0]
    half_rows = tile_rows // halves
    full_width = queries.shape[1]
    head_count = full_width // HD
    heads_dev = head_count // groups
    local_width = heads_dev * HD
    tile_count = loader_tiles.shape[0]
    image_count = image_tiles.shape[0]
    query_send = queries.reshape(halves, half_rows, groups, local_width).transpose(2, 0, 1, 3)
    query_send = query_send.reshape(seq_devices, half_rows, local_width)
    pair_parts = keys_values.reshape(tile_rows, 2, groups, local_width).transpose(2, 0, 1, 3)
    pair_send = jnp.broadcast_to(pair_parts[:, None], (groups, halves, tile_rows, 2, local_width))
    pair_send = pair_send.reshape(seq_devices, tile_rows, 2, local_width)
    query_got, pair_got = (
        lax.all_to_all(query_send, "seq", split_axis=0, concat_axis=0, tiled=True),
        lax.all_to_all(pair_send, "seq", split_axis=0, concat_axis=0, tiled=True),
    )
    position = jnp.arange(tile_count, dtype=jnp.int32)
    inverse = jnp.zeros((tile_count,), jnp.int32).at[loader_tiles].set(position)
    query_tiles = jnp.take(query_got, inverse, axis=0)
    pair_tiles = jnp.take(pair_got, inverse, axis=0)
    key_tiles = pair_tiles[:, :, 0].reshape(tile_count, tile_rows, heads_dev, HD)
    value_tiles = pair_tiles[:, :, 1].reshape(tile_count, tile_rows, heads_dev, HD)
    query_blocks = query_tiles.reshape(tile_count // 2, tile_rows, heads_dev, HD)
    image_ends = jnp.cumsum(image_tiles)
    image_starts = image_ends - image_tiles
    belongs = (
        (image_ends[None, :] > position[:, None]) & (image_starts[None, :] <= position[:, None])
    ).astype(jnp.int32)
    tile_image = jnp.sum(belongs * jnp.arange(image_count, dtype=jnp.int32)[None, :], axis=1)
    tile_start = jnp.sum(belongs * image_starts[None, :], axis=1)
    tile_stop = jnp.sum(belongs * image_ends[None, :], axis=1)
    score_scale = HD ** (-0.5)

    def one_block(inputs):
        query_block, block_index = inputs
        first_tile = 2 * block_index
        key_start = tile_start[first_tile]
        key_stop = tile_stop[first_tile + 1]
        row_image = jnp.concatenate(
            (
                jnp.full((half_rows,), tile_image[first_tile], jnp.int32),
                jnp.full((half_rows,), tile_image[first_tile + 1], jnp.int32),
            )
        )

        def key_step(key_tile_index, carry):
            row_best, row_total, weighted = carry
            key_tile = lax.dynamic_index_in_dim(key_tiles, key_tile_index, 0, keepdims=False)
            value_tile = lax.dynamic_index_in_dim(value_tiles, key_tile_index, 0, keepdims=False)
            scores = (
                jnp.einsum(
                    "qhd,khd->hqk", query_block, key_tile, preferred_element_type=jnp.float32
                )
                * score_scale
            )
            allowed = (row_image == tile_image[key_tile_index])[None, :, None]
            scores = jnp.where(allowed, scores, -1e30)
            new_best = jnp.maximum(row_best, jnp.max(scores, axis=2))
            weights = jnp.where(allowed, jnp.exp(scores - new_best[:, :, None]), 0.0)
            rescale = jnp.exp(row_best - new_best)
            row_total = row_total * rescale + jnp.sum(weights, axis=2)
            weighted = weighted * rescale[:, :, None] + jnp.einsum(
                "hqk,khd->hqd",
                weights.astype(jnp.bfloat16),
                value_tile,
                preferred_element_type=jnp.float32,
            )
            return (new_best, row_total, weighted)

        start_carry = (
            jnp.full((heads_dev, tile_rows), -1e30, jnp.float32),
            jnp.zeros((heads_dev, tile_rows), jnp.float32),
            jnp.zeros((heads_dev, tile_rows, HD), jnp.float32),
        )
        row_best, row_total, weighted = lax.fori_loop(key_start, key_stop, key_step, start_carry)
        result = weighted / row_total[:, :, None]
        return jnp.transpose(result, (1, 0, 2)).astype(jnp.bfloat16)

    outputs = lax.map(one_block, (query_blocks, jnp.arange(tile_count // 2, dtype=jnp.int32)))
    outputs = outputs.reshape(tile_count, half_rows, local_width)
    out_send = jnp.take(outputs, loader_tiles, axis=0)
    returned = lax.all_to_all(out_send, "seq", split_axis=0, concat_axis=0, tiled=True)
    returned = returned.reshape(groups, halves, half_rows, local_width).transpose(1, 2, 0, 3)
    return returned.reshape(tile_rows, full_width)


def solution(mesh):
    in_specs = (P(("dp", "seq"), None), P(("dp", "seq"), None, None), P("dp"), P("dp"))
    out_specs = P(("dp", "seq"), None)
    return jax.shard_map(local, mesh=mesh, in_specs=in_specs, out_specs=out_specs, check_vma=False)
```

profile of v0, /device:TPU:9, one launch (start us, length us, event | category | flops | bytes accessed | tf_op | source)
XLA Modules:
  0.0 950.1 jit_solution(14776244952594667061)
XLA Ops:
  4.4 8.6 all-to-all-start
  13.1 7.6 reshape.123
  26.4 14.5 %all-to-all-done = bf16[32,256,128]{2,1,0:T(8,128)(2,1)S(1)} async-done(((bf16[32,256,128]{2,1,0:T(8,128)(2,1)}), bf16[32,256,128]{2,1,0:T(8,128)(2,1)S(1)}, u32[]{:S(2)}, u32[]{:S(2)}) %all-to-all-start) | async-done | bytes 2097184 | tf_op jit(solution)/shard_map/all_to_all | solution.py:27
  40.9 8.3 broadcast_in_dim.76
  61.4 94.6 %all-to-all-done.1 = bf16[32,512,2,128]{3,1,2,0:T(8,128)(2,1)} async-done(((bf16[32,512,2,128]{3,1,2,0:T(8,128)(2,1)}), bf16[32,512,2,128]{3,1,2,0:T(8,128)(2,1)}, u32[]{:S(2)}, u32[]{:S(2)}) %all-to-all-start.1) | async-done | bytes 8388640 | tf_op jit(solution)/shard_map/all_to_all | solution.py:28
  156.0 8.4 gather_fusion
  177.7 728.6 %while.39 = (s32[]{:T(128)}, bf16[16,512,1,128]{3,1,2,0:T(8,128)(2,1)}, s32[16]{0:T(128)S(1)}, s32[32]{0:T(128)S(1)}, s32[32]{0:T(128)S(1)}, /*index=5*/bf16[16,...) while((s32[]{:T(128)}, ...), condition=%wide.region_10.12_spmd, body=%wide.region_5.0_spmd.sunk | while | flops 136840720 | bytes 5028988 | solution.py:92
  181.9 25.1 %while.40 = (s32[]{:T(128)}, f32[1,512]{1,0:T(1,128)S(1)}, f32[1,512]{1,0:T(1,128)S(1)}, f32[1,512,128]{2,1,0:T(8,128)S(1)}, s32[]{:T(128)}, /*index=5*/s32[32]{...) while((s32[]{:T(128)}, f32[1,512]{1,0:T(1,128)S(1)}, ...), condition=%wide.region_9.10_spmd, body=%wide.region_6.9_spmd.sunk | while | flops 136709632 | bytes 4100279 | solution.py:88
  212.0 81.0 %while.40 = (s32[]{:T(128)}, f32[1,512]{1,0:T(1,128)S(1)}, f32[1,512]{1,0:T(1,128)S(1)}, f32[1,512,128]{2,1,0:T(8,128)S(1)}, s32[]{:T(128)}, /*index=5*/s32[32]{...) while((s32[]{:T(128)}, f32[1,512]{1,0:T(1,128)S(1)}, ...), condition=%wide.region_9.10_spmd, body=%wide.region_6.9_spmd.sunk | while | flops 136709632 | bytes 4100279 | solution.py:88
  297.9 65.0 %while.40 = (s32[]{:T(128)}, f32[1,512]{1,0:T(1,128)S(1)}, f32[1,512]{1,0:T(1,128)S(1)}, f32[1,512,128]{2,1,0:T(8,128)S(1)}, s32[]{:T(128)}, /*index=5*/s32[32]{...) while((s32[]{:T(128)}, f32[1,512]{1,0:T(1,128)S(1)}, ...), condition=%wide.region_9.10_spmd, body=%wide.region_6.9_spmd.sunk | while | flops 136709632 | bytes 4100279 | solution.py:88
  367.9 65.0 %while.40 = (s32[]{:T(128)}, f32[1,512]{1,0:T(1,128)S(1)}, f32[1,512]{1,0:T(1,128)S(1)}, f32[1,512,128]{2,1,0:T(8,128)S(1)}, s32[]{:T(128)}, /*index=5*/s32[32]{...) while((s32[]{:T(128)}, f32[1,512]{1,0:T(1,128)S(1)}, ...), condition=%wide.region_9.10_spmd, body=%wide.region_6.9_spmd.sunk | while | flops 136709632 | bytes 4100279 | solution.py:88
  437.9 65.0 %while.40 = (s32[]{:T(128)}, f32[1,512]{1,0:T(1,128)S(1)}, f32[1,512]{1,0:T(1,128)S(1)}, f32[1,512,128]{2,1,0:T(8,128)S(1)}, s32[]{:T(128)}, /*index=5*/s32[32]{...) while((s32[]{:T(128)}, f32[1,512]{1,0:T(1,128)S(1)}, ...), condition=%wide.region_9.10_spmd, body=%wide.region_6.9_spmd.sunk | while | flops 136709632 | bytes 4100279 | solution.py:88
  507.9 81.0 %while.40 = (s32[]{:T(128)}, f32[1,512]{1,0:T(1,128)S(1)}, f32[1,512]{1,0:T(1,128)S(1)}, f32[1,512,128]{2,1,0:T(8,128)S(1)}, s32[]{:T(128)}, /*index=5*/s32[32]{...) while((s32[]{:T(128)}, f32[1,512]{1,0:T(1,128)S(1)}, ...), condition=%wide.region_9.10_spmd, body=%wide.region_6.9_spmd.sunk | while | flops 136709632 | bytes 4100279 | solution.py:88
  593.9 25.1 %while.40 = (s32[]{:T(128)}, f32[1,512]{1,0:T(1,128)S(1)}, f32[1,512]{1,0:T(1,128)S(1)}, f32[1,512,128]{2,1,0:T(8,128)S(1)}, s32[]{:T(128)}, /*index=5*/s32[32]{...) while((s32[]{:T(128)}, f32[1,512]{1,0:T(1,128)S(1)}, ...), condition=%wide.region_9.10_spmd, body=%wide.region_6.9_spmd.sunk | while | flops 136709632 | bytes 4100279 | solution.py:88
  623.9 17.1 %while.40 = (s32[]{:T(128)}, f32[1,512]{1,0:T(1,128)S(1)}, f32[1,512]{1,0:T(1,128)S(1)}, f32[1,512,128]{2,1,0:T(8,128)S(1)}, s32[]{:T(128)}, /*index=5*/s32[32]{...) while((s32[]{:T(128)}, f32[1,512]{1,0:T(1,128)S(1)}, ...), condition=%wide.region_9.10_spmd, body=%wide.region_6.9_spmd.sunk | while | flops 136709632 | bytes 4100279 | solution.py:88
  646.0 25.1 %while.40 = (s32[]{:T(128)}, f32[1,512]{1,0:T(1,128)S(1)}, f32[1,512]{1,0:T(1,128)S(1)}, f32[1,512,128]{2,1,0:T(8,128)S(1)}, s32[]{:T(128)}, /*index=5*/s32[32]{...) while((s32[]{:T(128)}, f32[1,512]{1,0:T(1,128)S(1)}, ...), condition=%wide.region_9.10_spmd, body=%wide.region_6.9_spmd.sunk | while | flops 136709632 | bytes 4100279 | solution.py:88
  676.1 33.1 %while.40 = (s32[]{:T(128)}, f32[1,512]{1,0:T(1,128)S(1)}, f32[1,512]{1,0:T(1,128)S(1)}, f32[1,512,128]{2,1,0:T(8,128)S(1)}, s32[]{:T(128)}, /*index=5*/s32[32]{...) while((s32[]{:T(128)}, f32[1,512]{1,0:T(1,128)S(1)}, ...), condition=%wide.region_9.10_spmd, body=%wide.region_6.9_spmd.sunk | while | flops 136709632 | bytes 4100279 | solution.py:88
  714.1 33.1 %while.40 = (s32[]{:T(128)}, f32[1,512]{1,0:T(1,128)S(1)}, f32[1,512]{1,0:T(1,128)S(1)}, f32[1,512,128]{2,1,0:T(8,128)S(1)}, s32[]{:T(128)}, /*index=5*/s32[32]{...) while((s32[]{:T(128)}, f32[1,512]{1,0:T(1,128)S(1)}, ...), condition=%wide.region_9.10_spmd, body=%wide.region_6.9_spmd.sunk | while | flops 136709632 | bytes 4100279 | solution.py:88
  752.2 25.1 %while.40 = (s32[]{:T(128)}, f32[1,512]{1,0:T(1,128)S(1)}, f32[1,512]{1,0:T(1,128)S(1)}, f32[1,512,128]{2,1,0:T(8,128)S(1)}, s32[]{:T(128)}, /*index=5*/s32[32]{...) while((s32[]{:T(128)}, f32[1,512]{1,0:T(1,128)S(1)}, ...), condition=%wide.region_9.10_spmd, body=%wide.region_6.9_spmd.sunk | while | flops 136709632 | bytes 4100279 | solution.py:88
  782.3 25.1 %while.40 = (s32[]{:T(128)}, f32[1,512]{1,0:T(1,128)S(1)}, f32[1,512]{1,0:T(1,128)S(1)}, f32[1,512,128]{2,1,0:T(8,128)S(1)}, s32[]{:T(128)}, /*index=5*/s32[32]{...) while((s32[]{:T(128)}, f32[1,512]{1,0:T(1,128)S(1)}, ...), condition=%wide.region_9.10_spmd, body=%wide.region_6.9_spmd.sunk | while | flops 136709632 | bytes 4100279 | solution.py:88
  812.3 41.1 %while.40 = (s32[]{:T(128)}, f32[1,512]{1,0:T(1,128)S(1)}, f32[1,512]{1,0:T(1,128)S(1)}, f32[1,512,128]{2,1,0:T(8,128)S(1)}, s32[]{:T(128)}, /*index=5*/s32[32]{...) while((s32[]{:T(128)}, f32[1,512]{1,0:T(1,128)S(1)}, ...), condition=%wide.region_9.10_spmd, body=%wide.region_6.9_spmd.sunk | while | flops 136709632 | bytes 4100279 | solution.py:88
  858.4 25.1 %while.40 = (s32[]{:T(128)}, f32[1,512]{1,0:T(1,128)S(1)}, f32[1,512]{1,0:T(1,128)S(1)}, f32[1,512,128]{2,1,0:T(8,128)S(1)}, s32[]{:T(128)}, /*index=5*/s32[32]{...) while((s32[]{:T(128)}, f32[1,512]{1,0:T(1,128)S(1)}, ...), condition=%wide.region_9.10_spmd, body=%wide.region_6.9_spmd.sunk | while | flops 136709632 | bytes 4100279 | solution.py:88
  888.5 17.1 %while.40 = (s32[]{:T(128)}, f32[1,512]{1,0:T(1,128)S(1)}, f32[1,512]{1,0:T(1,128)S(1)}, f32[1,512,128]{2,1,0:T(8,128)S(1)}, s32[]{:T(128)}, /*index=5*/s32[32]{...) while((s32[]{:T(128)}, f32[1,512]{1,0:T(1,128)S(1)}, ...), condition=%wide.region_9.10_spmd, body=%wide.region_6.9_spmd.sunk | while | flops 136709632 | bytes 4100279 | solution.py:88
  909.2 37.7 %all_to_all.15 = bf16[32,256,128]{2,1,0:T(8,128)(2,1)S(1)} all-to-all(bf16[32,256,128]{2,1,0:T(8,128)(2,1)S(1)} %broadcast_select_fusion.1), channel_id=1, replica_groups=mesh['seq'=32,'dp'=4] {'seq'}, dimensions={0} | all-to-all | bytes 4194304 | tf_op jit(solution)/shard_map/all_to_all | solution.py:95
  (840 shorter events, 426.7 us)
Async XLA Ops:
  4.4 36.5 %all-to-all-start = ((bf16[32,256,128]{2,1,0:T(8,128)(2,1)}), bf16[32,256,128]{2,1,0:T(8,128)(2,1)S(1)}, u32[]{:S(2)}, u32[]{:S(2)}) async-start(bf16[32,256,128]{2,1,0:T(8,128)(2,1)} %bitcast.93), calls=%async_computation | async-start | bytes 4194304 | tf_op jit(solution)/shard_map/all_to_all | solution.py:27
  49.2 7.1 copy-start
  49.2 7.3 copy-start.1
  49.2 106.8 %all-to-all-start.1 = ((bf16[32,512,2,128]{3,1,2,0:T(8,128)(2,1)}), bf16[32,512,2,128]{3,1,2,0:T(8,128)(2,1)}, u32[]{:S(2)}, u32[]{:S(2)}) async-start(bf16[32,512,2,128]{3,1,2,0:T(8,128)(2,1)} %bitcast.89), calls=%async_computation.1 | async-start | bytes 16777216 | tf_op jit(solution)/shard_map/all_to_all | solution.py:28
where the time goes:
time: 959 us; the launch traced here: 950 us
  loops' own time  344 us (36%)
  matrix products  200 us (21%)
  local copies, waits for them, and re-layouts  153 us (16%)
  waiting for transfers between devices  109 us (11%)
  other arithmetic  90.9 us (9%)
  blocking collectives  37.7 us (4%)
  starting transfers between devices  15.6 us (2%)
    another operation x16, loops' own time, one_block(): lax.fori_loop(key_start, key_stop, key_step, start_carry)  333 us
    dot_general x79, matrix products, key_step(): jnp.einsum('hqk,khd->hqd', weights.astype(jnp.bfloat16), value_tile, pref...  103 us
    dot_general x79, matrix products, key_step(): jnp.einsum('qhd,khd->hqk', query_block, key_tile, preferred_element_type=...  96.4 us
    all_to_all x1, waiting for transfers between devices, local(): lax.all_to_all(pair_send, 'seq', split_axis=0, concat_axis=0, tiled=True)  94.6 us
    eq x79, other arithmetic, key_step(): allowed = (row_image == tile_image[key_tile_index])[None, :, None]  49.7 us
    dynamic_slice x79, local copies, waits for them, and re-layouts, key_step(): allowed = (row_image == tile_image[key_tile_index])[None, :, None]  47.4 us
    all_to_all x1, blocking collectives, local(): lax.all_to_all(out_send, 'seq', split_axis=0, concat_axis=0, tiled=True)  37.7 us
  transfers between devices with their start and end apart: 2, of which 2 were waited for; matrix products, arithmetic and copies ran while one was open for 2% of the time, Pallas kernels for 0%

commit v1 on v0

v1 whole, which is shorter than its diff:
```python
import functools

import jax
import jax.numpy as jnp
from jax import lax
from jax.experimental import pallas as pl
from jax.experimental.pallas import tpu as pltpu
from jax.sharding import PartitionSpec as P

MESH = pl.DeviceIdType.MESH
HD = 128
HALF = 256
SIDE = 4
CHIPS = 16
DEVS = 32
MAXT = 8
STEPS = 150
UNROLL = 6
LISTS = 160
SCALE = HD**-0.5 * 1.4426950408889634
LOW = -1e30


def offset(n, core):
    m = ((15 - n) * 7) % CHIPS
    a, b = m // SIDE, m % SIDE
    return jnp.where(core == 0, a, b), jnp.where(core == 0, b, a)


def chip_at(chip, n, core, sign=1):
    dz, dx = offset(n, core)
    z, x = chip // SIDE, chip % SIDE
    return ((z + SIDE + sign * dz) % SIDE) * SIDE + (x + SIDE + sign * dx) % SIDE


def target(me, jj):
    core, chip = me % 2, me // 2
    n, e = jj // 2, jj % 2
    return chip_at(chip, n, core) * 2 + (core + 1 - e) % 2


def list_kernel(tiles_ref, loader_ref, qi_ref, kj_ref, first_ref, la_ref, last_ref, holder, begin, end):
    me = lax.axis_index("seq")

    def place(p, _):
        holder[loader_ref[p]] = p
        return 0

    lax.fori_loop(0, DEVS, place, 0)

    def image(m, start):
        stop = start + tiles_ref[m]

        def mark(t, _):
            begin[t] = start
            end[t] = stop
            return 0

        lax.fori_loop(start, stop, mark, 0)
        return stop

    lax.fori_loop(0, tiles_ref.shape[0], image, jnp.int32(0))

    def query(jj, s):
        p = target(me, jj)
        t = loader_ref[p]
        lo, hi = begin[t], end[t]
        stop = s + hi - lo

        def pair(t2, s):
            qi_ref[s] = p
            kj_ref[s] = holder[t2]
            first_ref[s] = (t2 == lo).astype(jnp.int32)
            la_ref[s] = stop - 1
            return s + 1

        s = lax.fori_loop(lo, hi, pair, s)
        last_ref[jj] = s - 1
        return s

    done = lax.fori_loop(0, DEVS, query, jnp.int32(0))

    def rest(s, _):
        qi_ref[s] = 0
        kj_ref[s] = 0
        first_ref[s] = 1
        la_ref[s] = 0
        return 0

    lax.fori_loop(done, LISTS, rest, 0)


def make_lists(image_tiles, loader_tiles):
    smem = pl.BlockSpec(memory_space=pltpu.SMEM)
    return pl.pallas_call(
        list_kernel,
        out_shape=[jax.ShapeDtypeStruct((LISTS,), jnp.int32)] * 4 + [jax.ShapeDtypeStruct((DEVS,), jnp.int32)],
        in_specs=[smem] * 2,
        out_specs=[smem] * 5,
        scratch_shapes=[pltpu.SMEM((DEVS,), jnp.int32)] * 3,
        name="lists",
    )(image_tiles, loader_tiles)


def dot_nt(a, b):
    return lax.dot_general(a, b, (((1,), (1,)), ((), ())), preferred_element_type=jnp.float32)


def dot_nn(a, b):
    return lax.dot_general(a, b, (((1,), (0,)), ((), ())), preferred_element_type=jnp.float32)


def attend_kernel(
    q_hbm,
    kv_hbm,
    qi,
    kj,
    first,
    la,
    last,
    out_hbm,
    pair,
    wide,
    stage,
    kv_a,
    kv_b,
    q,
    scores,
    probs,
    alpha,
    total,
    peak,
    slot_a,
    m_a,
    l_a,
    acc,
    slot_b,
    o_send,
    s_pair,
    s_q,
    r_q,
    s_kv,
    r_kv,
    s_fwd,
    s_o,
    r_o,
    s_own,
):
    me = lax.axis_index("seq")
    core, chip = me % 2, me // 2
    partner = chip * 2 + 1 - core
    kv = (kv_a, kv_b)

    def remote(src, dst, send, recv, device):
        return pltpu.make_async_remote_copy(
            src_ref=src, dst_ref=dst, send_sem=send, recv_sem=recv, device_id={"seq": device}, device_id_type=MESH
        )

    def cols(head):
        return pl.ds(pl.multiple_of(head * HD, HD), HD)

    def pair_load(head):
        return pltpu.make_async_copy(kv_hbm.at[:, :, cols(head)], pair.at[head], s_pair.at[head])

    def pair_loads(n, _):
        pair_load(chip_at(chip, n, core)).start()
        return 0

    lax.fori_loop(0, CHIPS, pair_loads, 0)

    barrier = pltpu.get_barrier_semaphore()
    for d in range(1, DEVS):
        pl.semaphore_signal(barrier, inc=1, device_id={"seq": (me + d) % DEVS}, device_id_type=MESH)
    pl.semaphore_wait(barrier, DEVS - 1)

    def q_copy(jj):
        device = target(me, jj)
        rows = pl.ds(pl.multiple_of((device % 2) * HALF, HALF), HALF)
        return remote(q_hbm.at[rows, cols(device // 2)], q.at[me], s_q.at[jj], r_q.at[me], device)

    def q_sends(jj, _):
        q_copy(jj).start()
        return 0

    lax.fori_loop(0, DEVS - 1, q_sends, 0)
    own_rows = pl.ds(pl.multiple_of(core * HALF, HALF), HALF)
    own_q = pltpu.make_async_copy(q_hbm.at[own_rows, cols(chip)], q.at[me], s_own.at[0])
    own_q.start()

    def kv_copy(u, n):
        t = chip_at(chip, n, core)
        return remote(stage.at[t, u], kv[u].at[me], s_kv.at[u, n], r_kv.at[u, me], t * 2 + core)

    def split(n, _):
        t = chip_at(chip, n, core)
        pair_load(t).wait()
        wide[...] = pair[t].reshape(2 * 2 * HALF, HD).astype(jnp.float32)
        keys = wide[pl.ds(0, 2 * HALF, stride=2), :].astype(jnp.bfloat16)
        values = wide[pl.ds(1, 2 * HALF, stride=2), :].T.astype(jnp.bfloat16)
        for u in range(2):
            stage[t, u, 0:HALF] = keys[u * HALF : (u + 1) * HALF]
            stage[t, u, HALF : HALF + HD] = values[:, u * HALF : u * HALF + HD]
            stage[t, u, HALF + HD : 2 * HALF] = values[:, u * HALF + HD : (u + 1) * HALF]

        @pl.when(n < CHIPS - 1)
        def _():
            kv_copy(0, n).start()

        return 0

    lax.fori_loop(0, CHIPS, split, 0)

    def kv_sends(n, _):
        kv_copy(1, n).start()
        return 0

    lax.fori_loop(0, CHIPS - 1, kv_sends, 0)
    own_kv = [pltpu.make_async_copy(stage.at[chip, u], kv[u].at[me], s_own.at[1 + u]) for u in range(2)]
    own_fwd = [
        remote(stage.at[chip, u], kv[u].at[me], s_fwd.at[u, CHIPS - 1], r_kv.at[u, me], partner) for u in range(2)
    ]
    for u in range(2):
        own_kv[u].start()
        own_fwd[u].start()

    def forward_copy(u, n):
        p = chip_at(chip, n, core, -1) * 2 + core
        return remote(kv[u].at[p], kv[u].at[p], s_fwd.at[u, n], r_kv.at[u, p], partner)

    def forward(u):
        def step(n, _):
            copy = forward_copy(u, n)
            copy.wait_recv()
            copy.start()
            return 0

        return step

    def kv_arrive(u):
        def step(c, _):
            p = c * 2 + 1 - core
            remote(kv[u].at[p], kv[u].at[p], s_fwd.at[u, 0], r_kv.at[u, p], partner).wait_recv()
            return 0

        lax.fori_loop(0, CHIPS, step, 0)

    lax.fori_loop(0, CHIPS - 1, forward(0), 0)

    def q_arrive(d, _):
        p = (me + d) % DEVS
        remote(q.at[p], q.at[p], s_q.at[0], r_q.at[p], partner).wait_recv()
        return 0

    lax.fori_loop(1, DEVS, q_arrive, 0)
    own_q.wait()
    own_kv[0].wait()
    kv_arrive(0)

    def stage_scores(u, s, w):
        sc = dot_nt(kv[u][kj[s], 0:HALF], q[qi[s]])
        scores[w] = sc
        peak[w] = jnp.max(sc, axis=0, keepdims=True) * SCALE

    def stage_weights(u, s, w, carry):
        m, l = carry
        new = first[s] == 1
        m = jnp.where(new, LOW if u == 0 else m_a[la[s]], m)
        l = jnp.where(new, 0.0 if u == 0 else l_a[la[s]], l)
        m_new = jnp.maximum(m, peak[w])
        p = jnp.exp2(scores[w] * SCALE - m_new)
        al = jnp.exp2(m - m_new)
        l = l * al + jnp.sum(p, axis=0, keepdims=True)
        probs[w] = p.astype(jnp.bfloat16)
        alpha[w] = al
        if u == 0:
            m_a[s] = m_new
            l_a[s] = l
        else:
            total[w] = l
        return m_new, l

    def stage_values(u, s, w):
        j = kj[s]
        d = dot_nn(kv[u][j, HALF : HALF + HD], probs[w, 0:HD]) + dot_nn(
            kv[u][j, HALF + HD : 2 * HALF], probs[w, HD : 2 * HD]
        )
        prev = acc[...]
        if u == 1:
            prev = jnp.where(first[s] == 1, slot_a[la[s]], prev)
        a = prev * alpha[w] + d
        acc[...] = a
        if u == 0:
            slot_a[s] = a
        else:
            slot_b[s] = (a * (1.0 / total[w])).astype(jnp.bfloat16)

    def attend(u, beside):
        ahead_s, ahead_w = 4, 2
        acc[...] = jnp.zeros_like(acc)
        carry = (jnp.zeros((1, HALF), jnp.float32), jnp.zeros((1, HALF), jnp.float32))
        for s in range(ahead_s):
            stage_scores(u, s, s)
        for s in range(ahead_w):
            carry = stage_weights(u, s, s, carry)

        def body(t, carry):
            for w in range(UNROLL):
                s = t * UNROLL + w
                stage_values(u, s, w)
                stage_scores(u, s + ahead_s, (w + ahead_s) % UNROLL)
                carry = stage_weights(u, s + ahead_w, (w + ahead_w) % UNROLL, carry)
            beside(t)
            return carry

        lax.fori_loop(0, STEPS // UNROLL, body, carry)

    def forwards_due(t):
        return jnp.clip(t - 8, 0, CHIPS - 1)

    def beside_a(t):
        lax.fori_loop(forwards_due(t), forwards_due(t + 1), forward(1), 0)

    attend(0, beside_a)
    own_kv[1].wait()
    kv_arrive(1)

    def o_copy(jj):
        out_rows = pl.ds(pl.multiple_of(core * HALF, HALF), HALF)
        return remote(o_send.at[jj], out_hbm.at[out_rows, cols(chip)], s_o.at[jj], r_o.at[me], target(me, jj))

    own_o = pltpu.make_async_copy(o_send.at[DEVS - 1], out_hbm.at[own_rows, cols(chip)], s_own.at[3])

    def emit(jj, _):
        o_send[jj] = slot_b[last[jj]].astype(jnp.float32).T.astype(jnp.bfloat16)

        @pl.when(jj < DEVS - 1)
        def _():
            o_copy(jj).start()

        @pl.when(jj == DEVS - 1)
        def _():
            own_o.start()

        return 0

    def outputs_due(t):
        s = t * UNROLL
        return jnp.clip(jnp.maximum(s // MAXT, s - (STEPS - DEVS)), 0, DEVS)

    def beside_b(t):
        lax.fori_loop(outputs_due(t), outputs_due(t + 1), emit, 0)

    attend(1, beside_b)

    def q_sent(jj, _):
        q_copy(jj).wait_send()
        return 0

    lax.fori_loop(0, DEVS - 1, q_sent, 0)
    for u in range(2):

        def kv_sent(n, _, u=u):
            kv_copy(u, n).wait_send()
            forward_copy(u, n).wait_send()
            return 0

        lax.fori_loop(0, CHIPS - 1, kv_sent, 0)
        own_fwd[u].wait_send()

    def o_sent(jj, _):
        o_copy(jj).wait_send()
        return 0

    lax.fori_loop(0, DEVS - 1, o_sent, 0)
    own_o.wait()

    def o_arrive(d, _):
        p = (me + d) % DEVS
        rows = pl.ds(pl.multiple_of((p % 2) * HALF, HALF), HALF)
        remote(o_send.at[0], out_hbm.at[rows, cols(p // 2)], s_o.at[0], r_o.at[p], partner).wait_recv()
        return 0

    lax.fori_loop(1, DEVS, o_arrive, 0)


def local(queries, keys_values, image_tiles, loader_tiles):
    lists = make_lists(image_tiles, loader_tiles)
    bf16, f32 = jnp.bfloat16, jnp.float32
    anywhere = pl.BlockSpec(memory_space=pl.ANY)
    smem = pl.BlockSpec(memory_space=pltpu.SMEM)
    dma = pltpu.SemaphoreType.DMA
    return pl.pallas_call(
        attend_kernel,
        out_shape=jax.ShapeDtypeStruct(queries.shape, bf16),
        in_specs=[anywhere] * 2 + [smem] * 5,
        out_specs=anywhere,
        scratch_shapes=[
            pltpu.VMEM((CHIPS, 2 * HALF, 2, HD), bf16),
            pltpu.VMEM((4 * HALF, HD), f32),
            pltpu.VMEM((CHIPS, 2, 2 * HALF, HD), bf16),
            pltpu.VMEM((DEVS, 2 * HALF, HD), bf16),
            pltpu.VMEM((DEVS, 2 * HALF, HD), bf16),
            pltpu.VMEM((DEVS, HALF, HD), bf16),
            pltpu.VMEM((UNROLL, HALF, HALF), f32),
            pltpu.VMEM((UNROLL, HALF, HALF), bf16),
            pltpu.VMEM((UNROLL, 1, HALF), f32),
            pltpu.VMEM((UNROLL, 1, HALF), f32),
            pltpu.VMEM((UNROLL, 1, HALF), f32),
            pltpu.VMEM((STEPS, HD, HALF), f32),
            pltpu.VMEM((LISTS, 1, HALF), f32),
            pltpu.VMEM((LISTS, 1, HALF), f32),
            pltpu.VMEM((HD, HALF), f32),
            pltpu.VMEM((STEPS, HD, HALF), bf16),
            pltpu.VMEM((DEVS, HALF, HD), bf16),
            dma((CHIPS,)),
            dma((DEVS,)),
            dma((DEVS,)),
            dma((2, CHIPS)),
            dma((2, DEVS)),
            dma((2, CHIPS)),
            dma((DEVS,)),
            dma((DEVS,)),
            dma((4,)),
        ],
        compiler_params=pltpu.CompilerParams(collective_id=0, has_side_effects=True, vmem_limit_bytes=62 << 20),
        name="attend",
    )(queries, keys_values, *lists)


def solution(mesh):
    in_specs = (P(("dp", "seq"), None), P(("dp", "seq"), None, None), P("dp"), P("dp"))
    out_specs = P(("dp", "seq"), None)
    return jax.shard_map(local, mesh=mesh, in_specs=in_specs, out_specs=out_specs, check_vma=False)
```

time: 959 us -> 127 us (0.13)
  loops' own time: 344 us -> 0 us
  matrix products: 200 us -> 0 us
  local copies, waits for them, and re-layouts: 153 us -> 3.16 us
  Pallas kernels: 0 us -> 123 us
  waiting for transfers between devices: 109 us -> 0 us
  other arithmetic: 90.9 us -> 0 us
  blocking collectives: 37.7 us -> 0 us
  starting transfers between devices: 15.6 us -> 0 us
    another operation x17 -> x0, loops' own time: 344 us -> none  [the longest x16 333 us: one_block(): lax.fori_loop(key_start, key_stop, key_step, start_carry)]
    dot_general x158 -> x0, matrix products: 200 us -> none  [the longest x79 103 us: key_step(): jnp.einsum('hqk,khd->hqd', weights.astype(jnp.bfloat16), value_tile, pref...]
    pallas_call x0 -> x2, Pallas kernels: none -> 123 us  [the longest x1 118 us: local(): pl.pallas_call(attend_kernel, out_shape=jax.ShapeDtypeStruct(queries.shap...]
    all_to_all x2 -> x0, waiting for transfers between devices: 109 us -> none  [the longest x1 94.6 us: local(): lax.all_to_all(pair_send, 'seq', split_axis=0, concat_axis=0, tiled=True)]
    dynamic_slice x143 -> x0, local copies, waits for them, and re-layouts: 84.4 us -> none  [the longest x79 47.4 us: key_step(): allowed = (row_image == tile_image[key_tile_index])[None, :, None]]
    eq x79 -> x0, other arithmetic: 49.7 us -> none  [key_step(): allowed = (row_image == tile_image[key_tile_index])[None, :, None]]
    all_to_all x1 -> x0, blocking collectives: 37.7 us -> none  [local(): lax.all_to_all(out_send, 'seq', split_axis=0, concat_axis=0, tiled=True)]
    broadcast_in_dim x17 -> x0, local copies, waits for them, and re-layouts: 18.3 us -> none  [the longest x16 10 us: one_block(): jnp.full((half_rows,), tile_image[first_tile], jnp.int32)]
  transfers between devices with their start and end apart: 2 -> 0, of which waited for: 2 -> 0; matrix products, arithmetic and copies ran while one was open for 2% -> 0% of each run, Pallas kernels for 0% -> 0%
where the time goes in v1:
time: 127 us; the launch traced here: 126 us
  Pallas kernels  123 us (97%)
  local copies, waits for them, and re-layouts  3.16 us (2%)
    pallas_call x1, Pallas kernels, local(): pl.pallas_call(attend_kernel, out_shape=jax.ShapeDtypeStruct(queries.shap...  118 us
    pallas_call x1, Pallas kernels, make_lists(): pl.pallas_call(list_kernel, out_shape=[jax.ShapeDtypeStruct((LISTS,), jnp...  4.81 us
    unnamed x1, local copies, waits for them, and re-layouts  3.16 us

profile of v1, /device:TPU:9, one launch (start us, length us, event | category | flops | bytes accessed | tf_op | source)
XLA Modules:
  0.0 126.2 jit_solution(14562905867287971245)
XLA Ops:
  0.0 4.8 %lists.1 = (s32[160]{0:T(256)}, s32[160]{0:T(256)}, s32[160]{0:T(256)}, s32[160]{0:T(256)}, s32[32]{0:T(128)}) custom-call(s32[16]{0:T(128)} %tiles_ref.1, s32[32]{0:T(128)} %loader_ref.1), custom_call_target="tpu_custom_call" | custom-call | tf_op jit(solution)/shard_map/lists/pallas_call | solution.py:95
  4.8 118.2 %attend.1 = bf16[512,2048]{1,0:T(8,128)(2,1)} custom-call(bf16[512,2048]{1,0:T(8,128)(2,1)} %q_hbm.1, bf16[512,2,2048]{2,1,0:T(2,128)(2,1)} %kv_hbm.1, s32[160]{0:T(256)} %get-tuple-element.10.qi, s32[160]{0:T(256)} %get-tuple-element.11.kj, s32[160]{0:T(256)} %get-tuple-element.12.first, s32[160]{0:T(256)} %get-tuple-element.13.la, s32[32]{0:T(128)} %get-tuple-element.14.last), custom_call_target="tpu_custom_call" | custom-call | tf_op jit(solution)/shard_map/attend/pallas_call | solution.py:392
  123.1 3.2 %copy.6 = bf16[512,2048]{1,0:T(8,128)(2,1)} copy(bf16[512,2048]{1,0:T(8,128)(2,1)} %attend.1) | data formatting | bytes 4194304

commit v2 on v1

--- a/solution.py
+++ b/solution.py
@@ -13,10 +13,11 @@
 SIDE = 4
 CHIPS = 16
 DEVS = 32
-MAXT = 8
-STEPS = 150
+MAX_UNITS = 4
+UNITS = 84
+MOST = 83
 UNROLL = 6
-LISTS = 160
+LISTS = 96
 SCALE = HD**-0.5 * 1.4426950408889634
 LOW = -1e30
 
@@ -39,67 +40,60 @@
     return chip_at(chip, n, core) * 2 + (core + 1 - e) % 2
 
 
-def list_kernel(tiles_ref, loader_ref, qi_ref, kj_ref, first_ref, la_ref, last_ref, holder, begin, end):
-    me = lax.axis_index("seq")
-
-    def place(p, _):
-        holder[loader_ref[p]] = p
+def fill_lists(me, tiles, loader, order, holder, begin, end, last, lists):
+    qi, k1, k2, pairs, first, la = lists
+    images = tiles.shape[0]
+
+    def place(t, _):
+        order[t] = target(me, t)
+        at = jnp.int32(0)
+        for p in range(DEVS):
+            at = at + jnp.where(loader[p] == t, p, 0)
+        holder[t] = at
         return 0
 
     lax.fori_loop(0, DEVS, place, 0)
 
-    def image(m, start):
-        stop = start + tiles_ref[m]
-
-        def mark(t, _):
-            begin[t] = start
-            end[t] = stop
-            return 0
-
-        lax.fori_loop(start, stop, mark, 0)
-        return stop
-
-    lax.fori_loop(0, tiles_ref.shape[0], image, jnp.int32(0))
-
-    def query(jj, s):
-        p = target(me, jj)
-        t = loader_ref[p]
+    def image(t, carry):
+        m, start, stop = carry
+        new = t == stop
+        m = jnp.where(new, jnp.minimum(m + 1, images - 1), m)
+        start = jnp.where(new, stop, start)
+        stop = jnp.where(new, stop + tiles[m], stop)
+        begin[t] = start
+        end[t] = stop
+        return m, start, stop
+
+    lax.fori_loop(0, DEVS, image, (jnp.int32(0), jnp.int32(0), tiles[0]))
+
+    def finish(jj, total):
+        t = loader[order[jj]]
+        size = end[t] - begin[t]
+        total = total + 1
+        for more in (2, 4, 6):
+            total = total + jnp.where(size > more, 1, 0)
+        last[jj] = jnp.minimum(total - 1, UNITS - 1)
+        return total
+
+    lax.fori_loop(0, DEVS, finish, jnp.int32(0))
+
+    def unit(s, carry):
+        jj, r = carry
+        p = order[jj]
+        t = loader[p]
         lo, hi = begin[t], end[t]
-        stop = s + hi - lo
-
-        def pair(t2, s):
-            qi_ref[s] = p
-            kj_ref[s] = holder[t2]
-            first_ref[s] = (t2 == lo).astype(jnp.int32)
-            la_ref[s] = stop - 1
-            return s + 1
-
-        s = lax.fori_loop(lo, hi, pair, s)
-        last_ref[jj] = s - 1
-        return s
-
-    done = lax.fori_loop(0, DEVS, query, jnp.int32(0))
-
-    def rest(s, _):
-        qi_ref[s] = 0
-        kj_ref[s] = 0
-        first_ref[s] = 1
-        la_ref[s] = 0
-        return 0
-
-    lax.fori_loop(done, LISTS, rest, 0)
-
-
-def make_lists(image_tiles, loader_tiles):
-    smem = pl.BlockSpec(memory_space=pltpu.SMEM)
-    return pl.pallas_call(
-        list_kernel,
-        out_shape=[jax.ShapeDtypeStruct((LISTS,), jnp.int32)] * 4 + [jax.ShapeDtypeStruct((DEVS,), jnp.int32)],
-        in_specs=[smem] * 2,
-        out_specs=[smem] * 5,
-        scratch_shapes=[pltpu.SMEM((DEVS,), jnp.int32)] * 3,
-        name="lists",
-    )(image_tiles, loader_tiles)
+        one = jnp.minimum(lo + 2 * r, hi - 1)
+        two = jnp.minimum(one + 1, hi - 1)
+        qi[s] = p
+        k1[s] = holder[one]
+        k2[s] = holder[two]
+        pairs[s] = two - one
+        first[s] = (r == 0).astype(jnp.int32)
+        la[s] = last[jj]
+        more = 2 * r + 2 < hi - lo
+        return jnp.where(more, jj, jnp.minimum(jj + 1, DEVS - 1)), jnp.where(more, r + 1, 0)
+
+    lax.fori_loop(0, LISTS, unit, (jnp.int32(0), jnp.int32(0)))
 
 
 def dot_nt(a, b):
@@ -113,11 +107,13 @@
 def attend_kernel(
     q_hbm,
     kv_hbm,
+    last,
     qi,
-    kj,
+    k1,
+    k2,
+    pairs,
     first,
     la,
-    last,
     out_hbm,
     pair,
     wide,
@@ -244,8 +240,6 @@
 
         lax.fori_loop(0, CHIPS, step, 0)
 
-    lax.fori_loop(0, CHIPS - 1, forward(0), 0)
-
     def q_arrive(d, _):
         p = (me + d) % DEVS
         remote(q.at[p], q.at[p], s_q.at[0], r_q.at[p], partner).wait_recv()
@@ -253,13 +247,18 @@
 
     lax.fori_loop(1, DEVS, q_arrive, 0)
     own_q.wait()
+
+    lax.fori_loop(0, CHIPS - 1, forward(0), 0)
     own_kv[0].wait()
     kv_arrive(0)
 
     def stage_scores(u, s, w):
-        sc = dot_nt(kv[u][kj[s], 0:HALF], q[qi[s]])
+        keys = jnp.concatenate([kv[u][k1[s], 0:HALF], kv[u][k2[s], 0:HALF]], axis=0)
+        sc = dot_nt(keys, q[qi[s]])
         scores[w] = sc
-        peak[w] = jnp.max(sc, axis=0, keepdims=True) * SCALE
+        one = jnp.max(sc[0:HALF], axis=0, keepdims=True)
+        two = jnp.max(sc[HALF : 2 * HALF], axis=0, keepdims=True)
+        peak[w] = jnp.where(pairs[s] == 1, jnp.maximum(one, two), one) * SCALE
 
     def stage_weights(u, s, w, carry):
         m, l = carry
@@ -267,10 +266,14 @@
         m = jnp.where(new, LOW if u == 0 else m_a[la[s]], m)
         l = jnp.where(new, 0.0 if u == 0 else l_a[la[s]], l)
         m_new = jnp.maximum(m, peak[w])
-        p = jnp.exp2(scores[w] * SCALE - m_new)
+        m_two = jnp.where(pairs[s] == 1, m_new, -LOW)
         al = jnp.exp2(m - m_new)
-        l = l * al + jnp.sum(p, axis=0, keepdims=True)
-        probs[w] = p.astype(jnp.bfloat16)
+        l = l * al
+        for x, m_x in enumerate((m_new, m_two)):
+            rows = pl.ds(x * HALF, HALF)
+            p = jnp.exp2(scores[w, rows] * SCALE - m_x)
+            l = l + jnp.sum(p, axis=0, keepdims=True)
+            probs[w, rows] = p.astype(jnp.bfloat16)
         alpha[w] = al
         if u == 0:
             m_a[s] = m_new
@@ -280,10 +283,8 @@
         return m_new, l
 
     def stage_values(u, s, w):
-        j = kj[s]
-        d = dot_nn(kv[u][j, HALF : HALF + HD], probs[w, 0:HD]) + dot_nn(
-            kv[u][j, HALF + HD : 2 * HALF], probs[w, HD : 2 * HD]
-        )
+        blocks = [kv[u][k[s], HALF + x * HD : HALF + (x + 1) * HD] for k in (k1, k2) for x in range(2)]
+        d = dot_nn(jnp.concatenate(blocks, axis=1), probs[w])
         prev = acc[...]
         if u == 1:
             prev = jnp.where(first[s] == 1, slot_a[la[s]], prev)
@@ -312,15 +313,16 @@
             beside(t)
             return carry
 
-        lax.fori_loop(0, STEPS // UNROLL, body, carry)
+        lax.fori_loop(0, UNITS // UNROLL, body, carry)
 
     def forwards_due(t):
-        return jnp.clip(t - 8, 0, CHIPS - 1)
+        return jnp.clip(t - 2, 0, CHIPS - 1)
 
     def beside_a(t):
         lax.fori_loop(forwards_due(t), forwards_due(t + 1), forward(1), 0)
 
     attend(0, beside_a)
+    lax.fori_loop(UNITS // UNROLL - 2, CHIPS - 1, forward(1), 0)
     own_kv[1].wait()
     kv_arrive(1)
 
@@ -345,7 +347,7 @@
 
     def outputs_due(t):
         s = t * UNROLL
-        return jnp.clip(jnp.maximum(s // MAXT, s - (STEPS - DEVS)), 0, DEVS)
+        return jnp.clip(jnp.maximum(s // MAX_UNITS, s - (MOST - DEVS)), 0, DEVS)
 
     def beside_b(t):
         lax.fori_loop(outputs_due(t), outputs_due(t + 1), emit, 0)
@@ -384,15 +386,27 @@
 
 
 def local(queries, keys_values, image_tiles, loader_tiles):
-    lists = make_lists(image_tiles, loader_tiles)
     bf16, f32 = jnp.bfloat16, jnp.float32
     anywhere = pl.BlockSpec(memory_space=pl.ANY)
     smem = pl.BlockSpec(memory_space=pltpu.SMEM)
     dma = pltpu.SemaphoreType.DMA
+
+    def list_kernel(tiles, loader, last, qi, k1, k2, pairs, first, la, order, holder, begin, end):
+        me = lax.axis_index("seq")
+        fill_lists(me, tiles, loader, order, holder, begin, end, last, (qi, k1, k2, pairs, first, la))
+
+    lists = pl.pallas_call(
+        list_kernel,
+        out_shape=[jax.ShapeDtypeStruct((DEVS,), jnp.int32)] + [jax.ShapeDtypeStruct((LISTS,), jnp.int32)] * 6,
+        in_specs=[smem] * 2,
+        out_specs=[smem] * 7,
+        scratch_shapes=[pltpu.SMEM((DEVS,), jnp.int32)] * 4,
+        name="lists",
+    )(image_tiles, loader_tiles)
     return pl.pallas_call(
         attend_kernel,
         out_shape=jax.ShapeDtypeStruct(queries.shape, bf16),
-        in_specs=[anywhere] * 2 + [smem] * 5,
+        in_specs=[anywhere] * 2 + [smem] * 7,
         out_specs=anywhere,
         scratch_shapes=[
             pltpu.VMEM((CHIPS, 2 * HALF, 2, HD), bf16),
@@ -401,16 +415,16 @@
             pltpu.VMEM((DEVS, 2 * HALF, HD), bf16),
             pltpu.VMEM((DEVS, 2 * HALF, HD), bf16),
             pltpu.VMEM((DEVS, HALF, HD), bf16),
-            pltpu.VMEM((UNROLL, HALF, HALF), f32),
-            pltpu.VMEM((UNROLL, HALF, HALF), bf16),
+            pltpu.VMEM((UNROLL, 2 * HALF, HALF), f32),
+            pltpu.VMEM((UNROLL, 2 * HALF, HALF), bf16),
             pltpu.VMEM((UNROLL, 1, HALF), f32),
             pltpu.VMEM((UNROLL, 1, HALF), f32),
             pltpu.VMEM((UNROLL, 1, HALF), f32),
-            pltpu.VMEM((STEPS, HD, HALF), f32),
+            pltpu.VMEM((UNITS, HD, HALF), f32),
             pltpu.VMEM((LISTS, 1, HALF), f32),
             pltpu.VMEM((LISTS, 1, HALF), f32),
             pltpu.VMEM((HD, HALF), f32),
-            pltpu.VMEM((STEPS, HD, HALF), bf16),
+            pltpu.VMEM((UNITS, HD, HALF), bf16),
             pltpu.VMEM((DEVS, HALF, HD), bf16),
             dma((CHIPS,)),
             dma((DEVS,)),

time: 127 us -> 128 us (level)
    pallas_call x1, Pallas kernels: 4.81 us -> 6.48 us  [local(): pl.pallas_call(list_kernel, out_shape=[jax.ShapeDtypeStruct((DEVS,), jnp....]
where the time goes in v2:
time: 128 us; the launch traced here: 127 us
  Pallas kernels  123 us (96%)
  local copies, waits for them, and re-layouts  3.16 us (2%)
    pallas_call x1, Pallas kernels, local(): pl.pallas_call(attend_kernel, out_shape=jax.ShapeDtypeStruct(queries.shap...  117 us
    pallas_call x1, Pallas kernels, local(): pl.pallas_call(list_kernel, out_shape=[jax.ShapeDtypeStruct((DEVS,), jnp....  6.48 us
    unnamed x1, local copies, waits for them, and re-layouts  3.16 us

profile of v2, /device:TPU:9, one launch (start us, length us, event | category | flops | bytes accessed | tf_op | source)
XLA Modules:
  0.0 126.7 jit_solution(18269005927165712917)
XLA Ops:
  0.0 6.5 %lists.1 = (s32[32]{0:T(128)}, s32[96]{0:T(128)}, s32[96]{0:T(128)}, s32[96]{0:T(128)}, s32[96]{0:T(128)}, /*index=5*/s32[96]{0:T(128)}, s32[96]{0:T(128)}) custom-call(s32[16]{0:T(128)} %tiles.1, s32[32]{0:T(128)} %loader.1), custom_call_target="tpu_custom_call" | custom-call | tf_op jit(solution)/shard_map/lists/pallas_call | solution.py:398
  6.5 117.0 %attend.1 = bf16[512,2048]{1,0:T(8,128)(2,1)} custom-call(bf16[512,2048]{1,0:T(8,128)(2,1)} %q_hbm.1, bf16[512,2,2048]{2,1,0:T(2,128)(2,1)} %kv_hbm.1, s32[32]{0:T(128)} %get-tuple-element.12.last, s32[96]{0:T(128)} %get-tuple-element.13.qi, s32[96]{0:T(128)} %get-tuple-element.14.k1, s32[96]{0:T(128)} %get-tuple-element.15.k2, s32[96]{0:T(128)} %get-tuple-element.16.pairs, ...), custom_call_target="tpu_custom_call" | custom-call | tf_op jit(solution)/shard_map/attend/pallas_call | solution.py:406
  123.5 3.2 %copy.6 = bf16[512,2048]{1,0:T(8,128)(2,1)} copy(bf16[512,2048]{1,0:T(8,128)(2,1)} %attend.1) | data formatting | bytes 4194304

commit v3 on v2

--- a/solution.py
+++ b/solution.py
@@ -17,14 +17,19 @@
 UNITS = 84
 MOST = 83
 UNROLL = 6
-LISTS = 96
+LISTS = 128
 SCALE = HD**-0.5 * 1.4426950408889634
 LOW = -1e30
 
 
+ORDER = ((2, 0), (0, 2), (2, 1), (2, 3), (1, 2), (3, 2), (2, 2), (1, 0), (3, 0), (0, 1), (0, 3), (1, 1), (3, 3), (1, 3), (3, 1))
+
+
 def offset(n, core):
-    m = ((15 - n) * 7) % CHIPS
-    a, b = m // SIDE, m % SIDE
+    a, b = jnp.zeros_like(n), jnp.zeros_like(n)
+    for k, (along_z, along_x) in enumerate(ORDER):
+        a = jnp.where(n == k, along_z, a)
+        b = jnp.where(n == k, along_x, b)
     return jnp.where(core == 0, a, b), jnp.where(core == 0, b, a)
 
 
@@ -40,64 +45,57 @@
     return chip_at(chip, n, core) * 2 + (core + 1 - e) % 2
 
 
-def fill_lists(me, tiles, loader, order, holder, begin, end, last, lists):
-    qi, k1, k2, pairs, first, la = lists
-    images = tiles.shape[0]
-
-    def place(t, _):
-        order[t] = target(me, t)
-        at = jnp.int32(0)
-        for p in range(DEVS):
-            at = at + jnp.where(loader[p] == t, p, 0)
-        holder[t] = at
-        return 0
-
-    lax.fori_loop(0, DEVS, place, 0)
-
-    def image(t, carry):
-        m, start, stop = carry
-        new = t == stop
-        m = jnp.where(new, jnp.minimum(m + 1, images - 1), m)
-        start = jnp.where(new, stop, start)
-        stop = jnp.where(new, stop + tiles[m], stop)
-        begin[t] = start
-        end[t] = stop
-        return m, start, stop
-
-    lax.fori_loop(0, DEVS, image, (jnp.int32(0), jnp.int32(0), tiles[0]))
-
-    def finish(jj, total):
-        t = loader[order[jj]]
-        size = end[t] - begin[t]
-        total = total + 1
-        for more in (2, 4, 6):
-            total = total + jnp.where(size > more, 1, 0)
-        last[jj] = jnp.minimum(total - 1, UNITS - 1)
-        return total
-
-    lax.fori_loop(0, DEVS, finish, jnp.int32(0))
-
-    def unit(s, carry):
-        jj, r = carry
-        p = order[jj]
-        t = loader[p]
-        lo, hi = begin[t], end[t]
-        one = jnp.minimum(lo + 2 * r, hi - 1)
-        two = jnp.minimum(one + 1, hi - 1)
-        qi[s] = p
-        k1[s] = holder[one]
-        k2[s] = holder[two]
-        pairs[s] = two - one
-        first[s] = (r == 0).astype(jnp.int32)
-        la[s] = last[jj]
-        more = 2 * r + 2 < hi - lo
-        return jnp.where(more, jj, jnp.minimum(jj + 1, DEVS - 1)), jnp.where(more, r + 1, 0)
-
-    lax.fori_loop(0, LISTS, unit, (jnp.int32(0), jnp.int32(0)))
-
-
-def dot_nt(a, b):
-    return lax.dot_general(a, b, (((1,), (1,)), ((), ())), preferred_element_type=jnp.float32)
+def list_kernel(tiles_ref, loader_ref, lists_ref):
+    me = lax.axis_index("seq")
+    f32 = jnp.float32
+    images = tiles_ref.shape[0]
+
+    def grid(shape, axis):
+        return lax.broadcasted_iota(jnp.int32, shape, axis)
+
+    def pick(mask, values, axis):
+        return jnp.sum(jnp.where(mask, values, 0.0), axis=axis, keepdims=True)
+
+    def across(ref):
+        n = ref.shape[0]
+        values = jnp.zeros((1, n), jnp.int32)
+        for i in range(n):
+            values = jnp.where(grid((1, n), 1) == i, ref[i], values)
+        return values.astype(f32)
+
+    tiles, loader = across(tiles_ref), across(loader_ref)
+    row, col = grid((DEVS, DEVS), 0), grid((DEVS, DEVS), 1)
+    image_row, image_col = grid((images, images), 0), grid((images, images), 1)
+    loader_down = pick(row == col, loader, 1)
+    tiles_down = pick(image_row == image_col, tiles, 1)
+    ends = pick(image_row <= image_col, tiles_down, 0)
+    starts = ends - tiles
+    place = target(me, grid((DEVS, 1), 0))
+    tile = pick(place == col, loader, 1)
+    lo, hi = pick(ends <= tile, tiles, 1), pick(starts <= tile, tiles, 1)
+    count = jnp.floor((hi - lo + 1.0) * 0.5)
+    after = pick(col <= row, pick(row == col, count, 0), 1)
+    before = after - count
+    s = grid((1, LISTS), 1).astype(f32)
+    mine = (before <= s) & (s < after)
+    r = s - pick(mine, before, 0)
+    one = pick(mine, lo, 0) + 2.0 * r
+    two = jnp.minimum(one + 1.0, pick(mine, hi, 0) - 1.0)
+    down = grid((DEVS, LISTS), 0)
+    devices = down.astype(f32)
+    live = s < jnp.sum(count, axis=0, keepdims=True)
+    lists = (
+        pick(mine, place.astype(f32), 0),
+        pick(loader_down == one, devices, 0),
+        pick(loader_down == two, devices, 0),
+        jnp.where(live, two - one, 0.0),
+        jnp.where(live, jnp.where(r == 0.0, 1.0, 0.0), 1.0),
+        pick(mine, after - 1.0, 0),
+        pick(down == grid((DEVS, LISTS), 1), after - 1.0, 0),
+    )
+    for i, values in enumerate(lists):
+        lists_ref[i : i + 1, :] = values.astype(jnp.int32)
+    lists_ref[len(lists) : len(lists) + 1, :] = jnp.zeros((1, LISTS), jnp.int32)
 
 
 def dot_nn(a, b):
@@ -107,13 +105,7 @@
 def attend_kernel(
     q_hbm,
     kv_hbm,
-    last,
-    qi,
-    k1,
-    k2,
-    pairs,
-    first,
-    la,
+    lists,
     out_hbm,
     pair,
     wide,
@@ -121,6 +113,7 @@
     kv_a,
     kv_b,
     q,
+    q_t,
     scores,
     probs,
     alpha,
@@ -146,6 +139,7 @@
     core, chip = me % 2, me // 2
     partner = chip * 2 + 1 - core
     kv = (kv_a, kv_b)
+    qi, k1, k2, pairs, first, la, last = [lists.at[i] for i in range(7)]
 
     def remote(src, dst, send, recv, device):
         return pltpu.make_async_remote_copy(
@@ -248,13 +242,18 @@
     lax.fori_loop(1, DEVS, q_arrive, 0)
     own_q.wait()
 
+    def turn(p, _):
+        q_t[p] = q[p].T
+        return 0
+
+    lax.fori_loop(0, DEVS, turn, 0)
     lax.fori_loop(0, CHIPS - 1, forward(0), 0)
     own_kv[0].wait()
     kv_arrive(0)
 
     def stage_scores(u, s, w):
         keys = jnp.concatenate([kv[u][k1[s], 0:HALF], kv[u][k2[s], 0:HALF]], axis=0)
-        sc = dot_nt(keys, q[qi[s]])
+        sc = dot_nn(keys, q_t[qi[s]])
         scores[w] = sc
         one = jnp.max(sc[0:HALF], axis=0, keepdims=True)
         two = jnp.max(sc[HALF : 2 * HALF], axis=0, keepdims=True)
@@ -391,22 +390,18 @@
     smem = pl.BlockSpec(memory_space=pltpu.SMEM)
     dma = pltpu.SemaphoreType.DMA
 
-    def list_kernel(tiles, loader, last, qi, k1, k2, pairs, first, la, order, holder, begin, end):
-        me = lax.axis_index("seq")
-        fill_lists(me, tiles, loader, order, holder, begin, end, last, (qi, k1, k2, pairs, first, la))
-
+    vmem = pl.BlockSpec(memory_space=pltpu.VMEM)
     lists = pl.pallas_call(
         list_kernel,
-        out_shape=[jax.ShapeDtypeStruct((DEVS,), jnp.int32)] + [jax.ShapeDtypeStruct((LISTS,), jnp.int32)] * 6,
+        out_shape=jax.ShapeDtypeStruct((8, LISTS), jnp.int32),
         in_specs=[smem] * 2,
-        out_specs=[smem] * 7,
-        scratch_shapes=[pltpu.SMEM((DEVS,), jnp.int32)] * 4,
+        out_specs=vmem,
         name="lists",
     )(image_tiles, loader_tiles)
     return pl.pallas_call(
         attend_kernel,
         out_shape=jax.ShapeDtypeStruct(queries.shape, bf16),
-        in_specs=[anywhere] * 2 + [smem] * 7,
+        in_specs=[anywhere] * 2 + [smem],
         out_specs=anywhere,
         scratch_shapes=[
             pltpu.VMEM((CHIPS, 2 * HALF, 2, HD), bf16),
@@ -415,6 +410,7 @@
             pltpu.VMEM((DEVS, 2 * HALF, HD), bf16),
             pltpu.VMEM((DEVS, 2 * HALF, HD), bf16),
             pltpu.VMEM((DEVS, HALF, HD), bf16),
+            pltpu.VMEM((DEVS, HD, HALF), bf16),
             pltpu.VMEM((UNROLL, 2 * HALF, HALF), f32),
             pltpu.VMEM((UNROLL, 2 * HALF, HALF), bf16),
             pltpu.VMEM((UNROLL, 1, HALF), f32),
@@ -436,9 +432,9 @@
             dma((DEVS,)),
             dma((4,)),
         ],
-        compiler_params=pltpu.CompilerParams(collective_id=0, has_side_effects=True, vmem_limit_bytes=62 << 20),
+        compiler_params=pltpu.CompilerParams(collective_id=0, has_side_effects=True, vmem_limit_bytes=48 << 20),
         name="attend",
-    )(queries, keys_values, *lists)
+    )(queries, keys_values, lists)
 
 
 def solution(mesh):

time: 128 us -> 121 us (0.945)
  Pallas kernels: 123 us -> 116 us
    pallas_call x1, Pallas kernels: 6.48 us -> 1.6 us  [local(): pl.pallas_call(list_kernel, out_shape=jax.ShapeDtypeStruct((8, LISTS), jn...]
    pallas_call x1, Pallas kernels: 117 us -> 114 us  [local(): pl.pallas_call(attend_kernel, out_shape=jax.ShapeDtypeStruct(queries.shap...]
    unnamed x1 -> x5, local copies, waits for them, and re-layouts: 3.16 us -> 3.6 us
where the time goes in v3:
time: 121 us; the launch traced here: 120 us
  Pallas kernels  116 us (96%)
  local copies, waits for them, and re-layouts  3.6 us (3%)
    pallas_call x1, Pallas kernels, local(): pl.pallas_call(attend_kernel, out_shape=jax.ShapeDtypeStruct(queries.shap...  114 us
    unnamed x5, local copies, waits for them, and re-layouts  3.6 us

profile of v3, /device:TPU:9, one launch (start us, length us, event | category | flops | bytes accessed | tf_op | source)
XLA Modules:
  0.0 119.6 jit_solution(314020005774707130)
XLA Ops:
  0.0 1.6 %lists.1 = s32[8,128]{1,0:T(8,128)} custom-call(s32[16]{0:T(128)} %tiles_ref.1, s32[32]{0:T(128)} %loader_ref.1), custom_call_target="tpu_custom_call" | custom-call | tf_op jit(solution)/shard_map/lists/pallas_call | solution.py:394
  1.6 0.0 copy-start
  1.6 1.6 %copy-done = bf16[512,2048]{1,0:T(8,128)(2,1)S(1)} copy-done((bf16[512,2048]{1,0:T(8,128)(2,1)S(1)}, bf16[512,2048]{1,0:T(8,128)(2,1)}, u32[]{:S(2)}) %copy-start) | copy-done | bytes 2097176
  3.2 0.0 copy-start.1
  3.2 0.7 copy-done.1
  3.9 114.4 %attend.1 = bf16[512,2048]{1,0:T(8,128)(2,1)S(1)} custom-call(bf16[512,2048]{1,0:T(8,128)(2,1)S(1)} %copy-done, bf16[512,2,2048]{2,1,0:T(2,128)(2,1)} %kv_hbm.1, s32[8,128]{1,0:T(8,128)S(1)} %copy-done.1), custom_call_target="tpu_custom_call" | custom-call | tf_op jit(solution)/shard_map/attend/pallas_call | solution.py:401
  118.2 1.3 %copy.6 = bf16[512,2048]{1,0:T(8,128)(2,1)} copy(bf16[512,2048]{1,0:T(8,128)(2,1)S(1)} %attend.1) | data formatting | bytes 4194304
Async XLA Ops:
  1.6 1.6 %copy-start = (bf16[512,2048]{1,0:T(8,128)(2,1)S(1)}, bf16[512,2048]{1,0:T(8,128)(2,1)}, u32[]{:S(2)}) copy-start(bf16[512,2048]{1,0:T(8,128)(2,1)} %q_hbm.1) | copy-start | bytes 6291460
  3.2 0.7 copy-start.1

commit v4 on v3

--- a/solution.py
+++ b/solution.py
@@ -292,7 +292,7 @@
         if u == 0:
             slot_a[s] = a
         else:
-            slot_b[s] = (a * (1.0 / total[w])).astype(jnp.bfloat16)
+            slot_b[s] = (a * (1.0 / total[w])).T.astype(jnp.bfloat16)
 
     def attend(u, beside):
         ahead_s, ahead_w = 4, 2
@@ -332,7 +332,7 @@
     own_o = pltpu.make_async_copy(o_send.at[DEVS - 1], out_hbm.at[own_rows, cols(chip)], s_own.at[3])
 
     def emit(jj, _):
-        o_send[jj] = slot_b[last[jj]].astype(jnp.float32).T.astype(jnp.bfloat16)
+        o_send[jj] = slot_b[last[jj]]
 
         @pl.when(jj < DEVS - 1)
         def _():
@@ -420,7 +420,7 @@
             pltpu.VMEM((LISTS, 1, HALF), f32),
             pltpu.VMEM((LISTS, 1, HALF), f32),
             pltpu.VMEM((HD, HALF), f32),
-            pltpu.VMEM((UNITS, HD, HALF), bf16),
+            pltpu.VMEM((UNITS, HALF, HD), bf16),
             pltpu.VMEM((DEVS, HALF, HD), bf16),
             dma((CHIPS,)),
             dma((DEVS,)),
@@ -432,7 +432,7 @@
             dma((DEVS,)),
             dma((4,)),
         ],
-        compiler_params=pltpu.CompilerParams(collective_id=0, has_side_effects=True, vmem_limit_bytes=48 << 20),
+        compiler_params=pltpu.CompilerParams(collective_id=0, has_side_effects=True, vmem_limit_bytes=51 << 20),
         name="attend",
     )(queries, keys_values, lists)
 

time: 121 us -> 119 us (0.983)
  local copies, waits for them, and re-layouts: 3.6 us -> 2.01 us
    unnamed x5 -> x3, local copies, waits for them, and re-layouts: 3.6 us -> 2.01 us
where the time goes in v4:
time: 119 us; the launch traced here: 118 us
  Pallas kernels  116 us (97%)
  local copies, waits for them, and re-layouts  2.01 us (2%)
    pallas_call x1, Pallas kernels, local(): pl.pallas_call(attend_kernel, out_shape=jax.ShapeDtypeStruct(queries.shap...  114 us

profile of v4, /device:TPU:9, one launch (start us, length us, event | category | flops | bytes accessed | tf_op | source)
XLA Modules:
  0.0 117.5 jit_solution(3159384837863845985)
XLA Ops:
  0.0 1.6 %lists.1 = s32[8,128]{1,0:T(8,128)} custom-call(s32[16]{0:T(128)} %tiles_ref.1, s32[32]{0:T(128)} %loader_ref.1), custom_call_target="tpu_custom_call" | custom-call | tf_op jit(solution)/shard_map/lists/pallas_call | solution.py:394
  1.6 0.0 copy-start
  1.6 0.7 copy-done
  2.3 113.9 %attend.1 = bf16[512,2048]{1,0:T(8,128)(2,1)S(1)} custom-call(bf16[512,2048]{1,0:T(8,128)(2,1)} %q_hbm.1, bf16[512,2,2048]{2,1,0:T(2,128)(2,1)} %kv_hbm.1, s32[8,128]{1,0:T(8,128)S(1)} %copy-done), custom_call_target="tpu_custom_call" | custom-call | tf_op jit(solution)/shard_map/attend/pallas_call | solution.py:401
  116.2 1.3 %copy.6 = bf16[512,2048]{1,0:T(8,128)(2,1)} copy(bf16[512,2048]{1,0:T(8,128)(2,1)S(1)} %attend.1) | data formatting | bytes 4194304
Async XLA Ops:
  1.6 0.7 copy-start

commit v5 on v4

--- a/solution.py
+++ b/solution.py
@@ -22,7 +22,7 @@
 LOW = -1e30
 
 
-ORDER = ((2, 0), (0, 2), (2, 1), (2, 3), (1, 2), (3, 2), (2, 2), (1, 0), (3, 0), (0, 1), (0, 3), (1, 1), (3, 3), (1, 3), (3, 1))
+ORDER = ((2, 2), (2, 1), (2, 3), (1, 2), (3, 2), (2, 0), (0, 2), (1, 1), (3, 3), (1, 3), (3, 1), (1, 0), (3, 0), (0, 1), (0, 3))
 
 
 def offset(n, core):

time: 119 us -> 124 us (1.042)
  Pallas kernels: 116 us -> 121 us
    pallas_call x1, Pallas kernels: 114 us -> 119 us  [local(): pl.pallas_call(attend_kernel, out_shape=jax.ShapeDtypeStruct(queries.shap...]
where the time goes in v5:
time: 124 us; the launch traced here: 123 us
  Pallas kernels  121 us (98%)
  local copies, waits for them, and re-layouts  2.01 us (2%)
    pallas_call x1, Pallas kernels, local(): pl.pallas_call(attend_kernel, out_shape=jax.ShapeDtypeStruct(queries.shap...  119 us

profile of v5, /device:TPU:9, one launch (start us, length us, event | category | flops | bytes accessed | tf_op | source)
XLA Modules:
  0.0 122.9 jit_solution(10859564022108774033)
XLA Ops:
  0.0 1.6 %lists.1 = s32[8,128]{1,0:T(8,128)} custom-call(s32[16]{0:T(128)} %tiles_ref.1, s32[32]{0:T(128)} %loader_ref.1), custom_call_target="tpu_custom_call" | custom-call | tf_op jit(solution)/shard_map/lists/pallas_call | solution.py:394
  1.6 0.0 copy-start
  1.6 0.7 copy-done
  2.3 119.3 %attend.1 = bf16[512,2048]{1,0:T(8,128)(2,1)S(1)} custom-call(bf16[512,2048]{1,0:T(8,128)(2,1)} %q_hbm.1, bf16[512,2,2048]{2,1,0:T(2,128)(2,1)} %kv_hbm.1, s32[8,128]{1,0:T(8,128)S(1)} %copy-done), custom_call_target="tpu_custom_call" | custom-call | tf_op jit(solution)/shard_map/attend/pallas_call | solution.py:401
  121.6 1.3 %copy.6 = bf16[512,2048]{1,0:T(8,128)(2,1)} copy(bf16[512,2048]{1,0:T(8,128)(2,1)S(1)} %attend.1) | data formatting | bytes 4194304
Async XLA Ops:
  1.6 0.7 copy-start

commit v6 on v4

--- a/solution.py
+++ b/solution.py
@@ -30,7 +30,7 @@
     for k, (along_z, along_x) in enumerate(ORDER):
         a = jnp.where(n == k, along_z, a)
         b = jnp.where(n == k, along_x, b)
-    return jnp.where(core == 0, a, b), jnp.where(core == 0, b, a)
+    return jnp.where(core == 0, a, (SIDE - b) % SIDE), jnp.where(core == 0, b, (SIDE - a) % SIDE)
 
 
 def chip_at(chip, n, core, sign=1):

time: 119 us -> 118 us (level)
  no operation moved by 1% of the time
where the time goes in v6:
time: 118 us; the launch traced here: 117 us
  Pallas kernels  115 us (97%)
  local copies, waits for them, and re-layouts  2.01 us (2%)
    pallas_call x1, Pallas kernels, local(): pl.pallas_call(attend_kernel, out_shape=jax.ShapeDtypeStruct(queries.shap...  113 us

profile of v6, /device:TPU:9, one launch (start us, length us, event | category | flops | bytes accessed | tf_op | source)
XLA Modules:
  0.0 117.1 jit_solution(111656787790417866)
XLA Ops:
  0.0 1.6 %lists.1 = s32[8,128]{1,0:T(8,128)} custom-call(s32[16]{0:T(128)} %tiles_ref.1, s32[32]{0:T(128)} %loader_ref.1), custom_call_target="tpu_custom_call" | custom-call | tf_op jit(solution)/shard_map/lists/pallas_call | solution.py:394
  1.6 0.0 copy-start
  1.6 0.7 copy-done
  2.3 113.4 %attend.1 = bf16[512,2048]{1,0:T(8,128)(2,1)S(1)} custom-call(bf16[512,2048]{1,0:T(8,128)(2,1)} %q_hbm.1, bf16[512,2,2048]{2,1,0:T(2,128)(2,1)} %kv_hbm.1, s32[8,128]{1,0:T(8,128)S(1)} %copy-done), custom_call_target="tpu_custom_call" | custom-call | tf_op jit(solution)/shard_map/attend/pallas_call | solution.py:401
  115.7 1.3 %copy.6 = bf16[512,2048]{1,0:T(8,128)(2,1)} copy(bf16[512,2048]{1,0:T(8,128)(2,1)S(1)} %attend.1) | data formatting | bytes 4194304
Async XLA Ops:
  1.6 0.7 copy-start
